TPU v7x, 32 devices: a whole 2x2x4 slice. The times are simulated.
32 devices in a mesh: group: 2 (over x), space: 16 (over z, y, core).
Axes of the slice: x: 2, y: 2, z: 4, core: 2. Of those that a mesh axis runs over, the one named last changes fastest.
Arguments:
- snapshots: bfloat16 [32, 3, 256, 128], P('group', None, 'space'), parts along dimension 0, may hold values from -8 to 8
- basis: bfloat16 [128, 3, 128, 256], P('group', None, 'space'), parts along dimension 0, may hold values from -6 to 6
- mode_weights: float32 [128], P('group'), parts along dimension 0, may hold values from 0.5 to 4
- land_mask: int32 [256, 128], P('space'), may hold values 0 or 1
- scale_index: int32 [128], replicated, may hold values from 0 to 15
- scale_values: float32 [16], replicated, may hold values from 0.06 to 0.24
Outputs:
- new_basis: bfloat16 [128, 3, 128, 256], P('group', None, 'space'), parts along dimension 0
- coefficients: float32 [32, 64], P('group'), parts along dimension 0
There are 2 independent parts, one for each index of `group`. A program takes and returns all parts, laid end to end along the dimension named above; an argument that names none is the same for every part. Nothing has to cross between parts.
Inputs may be any that keep to these rules, and one draw needn't show every extreme that they name: `land_mask`: 1 marks ocean, 0 land. Row y uses scale_values[scale_index[y]].
All inputs are finite; a program needn't handle non-finite values. No bound on the sum of `land_mask` on one device may be relied on, other than what follows from the above.
Results may differ from a plain program's by a relative error of at most 0.0057.
Values may be sent and summed in bfloat16 or wider, within the bound.
A program may use at most 128 MiB of HBM per device.

v0:
```python
import math
import jax
import jax.numpy as jnp
from jax import lax
from jax.sharding import PartitionSpec as P

PASS_COEFS = (1.0, 0.95, 0.85, 0.7, 0.5, 0.3)


def with_halo(cells, sides, width):
    for axis, dim in sides:
        count = lax.axis_size(axis)
        head = lax.slice_in_dim(cells, 0, width, axis=dim)
        tail = lax.slice_in_dim(cells, cells.shape[dim] - width, cells.shape[dim], axis=dim)
        cells = jnp.concatenate(
            [
                lax.ppermute(tail, axis, [(i, (i + 1) % count) for i in range(count)]),
                cells,
                lax.ppermute(head, axis, [((i + 1) % count, i) for i in range(count)]),
            ],
            axis=dim,
        )
    return cells


def latitude_scale(scale_index, scale_values):
    levels = jnp.arange(scale_values.shape[0], dtype=jnp.int32)
    matches = (scale_index[None, :] == levels[:, None]).astype(jnp.float32)
    return jnp.sum(matches * scale_values[:, None], axis=0)


def masked_step(fields_now, ocean, factor):
    centre = fields_now[:, :, 1:-1]
    m_centre = ocean[1:-1]
    east_flux = ocean[2:] * (fields_now[:, :, 2:] - centre)
    west_flux = ocean[:-2] * (fields_now[:, :, :-2] - centre)
    padded = jnp.pad(centre, ((0, 0), (0, 0), (0, 0), (1, 1)))
    m_pad = jnp.pad(m_centre, ((0, 0), (1, 1)))
    north_flux = m_pad[:, 2:] * (padded[..., 2:] - centre)
    south_flux = m_pad[:, :-2] * (padded[..., :-2] - centre)
    return centre + factor * (m_centre * (east_flux + west_flux + north_flux + south_flux))


def dot_rows(left, right):
    return lax.dot_general(
        left, right, (((1,), (1,)), ((), ())), preferred_element_type=jnp.float32
    )


def eof_update(data_rows, basis_rows, mode_weights, total_cells):
    high = lax.Precision.HIGHEST
    root_total = math.sqrt(total_cells)
    cross_sum = lax.psum(dot_rows(data_rows, basis_rows), "space")
    coefficients = cross_sum / root_total
    coeff_b = coefficients.astype(jnp.bfloat16)
    update = mode_weights[:, None] * basis_rows.astype(jnp.float32) + lax.dot_general(
        coeff_b, data_rows, (((0,), (0,)), ((), ())), preferred_element_type=jnp.float32
    )
    gram_matrix = lax.psum(jnp.dot(update, update.T, precision=high), "space") / total_cells
    chol_factor = jnp.linalg.cholesky(gram_matrix)
    solved = jax.scipy.linalg.solve_triangular(chol_factor, update, lower=True)
    return (solved.astype(jnp.bfloat16), coefficients)


def local(snapshots, basis, mode_weights, land_mask, scale_index, scale_values):
    lat_scale = latitude_scale(scale_index, scale_values)
    halo_width = 1
    ocean_wide = with_halo(land_mask, (("space", 0),), halo_width).astype(jnp.float32)
    fields_now = snapshots.astype(jnp.float32)
    for group_start in range(0, len(PASS_COEFS), halo_width):
        extended = with_halo(fields_now, (("space", 2),), 1)
        factor = PASS_COEFS[group_start] * lat_scale
        extended = masked_step(extended, ocean_wide, factor)
        fields_now = extended
    ocean = land_mask.astype(jnp.float32)
    filtered = (ocean * fields_now).astype(jnp.bfloat16)
    modes = basis.shape[0]
    snaps = filtered.shape[0]
    slab_data = lax.all_to_all(filtered, "space", split_axis=3, concat_axis=2, tiled=True)
    data_rows = jnp.swapaxes(slab_data, 2, 3).reshape(snaps, -1)
    basis_rows = basis.reshape(modes, -1)
    total_cells = float(data_rows.shape[1] * lax.axis_size("space"))
    solved, coefficients = eof_update(data_rows, basis_rows, mode_weights, total_cells)
    new_basis = solved.reshape(basis.shape)
    return (new_basis, coefficients)


def solution(mesh):
    placed = (
        P("group", None, "space", None),
        P("group", None, "space", None),
        P("group"),
        P("space", None),
        P(),
        P(),
    )
    return jax.shard_map(
        local,
        mesh=mesh,
        in_specs=placed,
        out_specs=(P("group", None, "space", None), P("group", None)),
        check_vma=False,
    )
```

profile of v0, /device:TPU:0, one launch (start us, length us, event | category | flops | bytes accessed | tf_op | source)
XLA Modules:
  0.0 175.6 jit_solution(13503581497344326809)
XLA Ops:
  0.6 0.7 fusion.94
  1.8 5.0 %collective-permute-start.1 = (s32[1,128]{1,0:T(1,128)S(1)}, s32[1,128]{1,0:T(1,128)S(1)}, u32[]{:S(2)}, u32[]{:S(2)}) collective-permute-start(s32[1,128]{1,0:T(1,128)S(1)} %get-tuple-element.20), channel_id=1, source_target_pairs={{1,0},{2,1},{3,2},{4,3},{5,4},{6,5},{7,6},{8,7},{9,8},{10,9},{11,1... | collective-permute-start | bytes 1544 | tf_op jit(solution)/shard_map/ppermute | solution.py:19
  6.8 1.0 copy_convert_fusion
  7.8 0.7 collective-permute-start.2
  8.5 0.7 add_convert_fusion
  9.2 0.8 pad_slice_fusion.13
  10.0 4.4 %collective-permute-done.3 = f32[16,3,1,128]{3,0,2,1:T(8,128)S(1)} collective-permute-done((f32[16,3,1,128]{3,0,2,1:T(8,128)S(1)}, f32[16,3,1,128]{3,0,2,1:T(8,128)S(1)}, u32[]{:S(2)}, u32[]{:S(2)}) %collective-permute-start.3) | collective-permute-done | bytes 24608 | tf_op jit(solution)/shard_map/ppermute | solution.py:17
  14.4 1.2 convert_add_fusion
  16.3 1.0 collective-permute-done.4
  17.3 4.6 %collective-permute-done.5 = f32[16,3,1,128]{3,0,2,1:T(8,128)S(1)} collective-permute-done((f32[16,3,1,128]{3,0,2,1:T(8,128)S(1)}, f32[16,3,1,128]{3,0,2,1:T(8,128)S(1)}, u32[]{:S(2)}, u32[]{:S(2)}) %collective-permute-start.5) | collective-permute-done | bytes 24608 | tf_op jit(solution)/shard_map/ppermute | solution.py:17
  22.7 1.0 collective-permute-done.6
  23.7 4.5 %collective-permute-done.7 = f32[16,3,1,128]{3,0,2,1:T(8,128)S(1)} collective-permute-done((f32[16,3,1,128]{3,0,2,1:T(8,128)S(1)}, f32[16,3,1,128]{3,0,2,1:T(8,128)S(1)}, u32[]{:S(2)}, u32[]{:S(2)}) %collective-permute-start.7) | collective-permute-done | bytes 24608 | tf_op jit(solution)/shard_map/ppermute | solution.py:17
  29.1 1.0 collective-permute-done.8
  30.1 4.5 %collective-permute-done.9 = f32[16,3,1,128]{3,0,2,1:T(8,128)S(1)} collective-permute-done((f32[16,3,1,128]{3,0,2,1:T(8,128)S(1)}, f32[16,3,1,128]{3,0,2,1:T(8,128)S(1)}, u32[]{:S(2)}, u32[]{:S(2)}) %collective-permute-start.9) | collective-permute-done | bytes 24608 | tf_op jit(solution)/shard_map/ppermute | solution.py:17
  35.5 1.0 collective-permute-done.10
  36.6 4.5 %collective-permute-done.11 = f32[16,3,1,128]{3,0,2,1:T(8,128)S(1)} collective-permute-done((f32[16,3,1,128]{3,0,2,1:T(8,128)S(1)}, f32[16,3,1,128]{3,0,2,1:T(8,128)S(1)}, u32[]{:S(2)}, u32[]{:S(2)}) %collective-permute-start.11) | collective-permute-done | bytes 24608 | tf_op jit(solution)/shard_map/ppermute | solution.py:17
  42.0 1.0 collective-permute-done.12
  43.0 4.5 %collective-permute-done.13 = f32[16,3,1,128]{3,0,2,1:T(8,128)S(1)} collective-permute-done((f32[16,3,1,128]{3,0,2,1:T(8,128)S(1)}, f32[16,3,1,128]{3,0,2,1:T(8,128)S(1)}, u32[]{:S(2)}, u32[]{:S(2)}) %collective-permute-start.13) | collective-permute-done | bytes 24608 | tf_op jit(solution)/shard_map/ppermute | solution.py:17
  47.8 1.1 copy.41
  48.9 2.3 %reshape.52 = bf16[16,2,3072]{2,1,0:T(2,128)(2,1)} reshape(bf16[128,3,16,16]{3,2,1,0:T(8,128)(2,1)S(1)} %bitcast.42) | data formatting | bytes 393216
  51.2 3.5 %all-to-all-start = ((bf16[16,2,3072]{2,1,0:T(2,128)(2,1)}), bf16[16,2,3072]{2,1,0:T(2,128)(2,1)S(1)}, u32[]{:S(2)}, u32[]{:S(2)}) async-start(bf16[16,2,3072]{2,1,0:T(2,128)(2,1)} %reshape.52), calls=%async_computation | async-start | bytes 393216 | tf_op jit(solution)/shard_map/all_to_all | solution.py:79
  54.9 8.8 %all-to-all-done = bf16[16,2,3072]{2,1,0:T(2,128)(2,1)S(1)} async-done(((bf16[16,2,3072]{2,1,0:T(2,128)(2,1)}), bf16[16,2,3072]{2,1,0:T(2,128)(2,1)S(1)}, u32[]{:S(2)}, u32[]{:S(2)}) %all-to-all-start) | async-done | bytes 196640 | tf_op jit(solution)/shard_map/all_to_all | solution.py:79
  63.7 1.2 reshape.53
  64.9 2.2 %copy.43 = bf16[16,3,16,16,8]{3,2,0,4,1:T(8,128)(2,1)} copy(bf16[16,3,16,16,8]{3,0,1,4,2:T(8,128)(2,1)S(1)} %bitcast.43) | data formatting | bytes 393216 | tf_op jit(solution)/shard_map/all_to_all | solution.py:79
  67.1 2.7 %all_to_all.16 = bf16[16,3,256,8]{2,0,3,1:T(8,128)(2,1)S(1)} reshape(bf16[16,3,16,16,8]{3,2,0,4,1:T(8,128)(2,1)} %copy.43) | data formatting | bytes 393216 | tf_op jit(solution)/shard_map/all_to_all | solution.py:79
  70.1 31.0 %psum.14 = f32[16,64]{1,0:T(8,128)S(1)} all-reduce(f32[16,64]{1,0:T(8,128)S(1)} %convolution_bitcast_fusion), channel_id=1, replica_groups=mesh['group'=2,'space'=16] {'space'}, use_global_device_ids=true, to_apply=%region_1.2 | all-reduce | flops 1024 | bytes 8192 | tf_op jit(solution)/shard_map/psum | solution.py:53
  101.7 1.4 fusion.95
  103.1 57.8 %psum.15 = f32[64,64]{0,1:T(8,128)S(1)} all-reduce(f32[64,64]{0,1:T(8,128)S(1)} %fusion.95), channel_id=1, replica_groups=mesh['group'=2,'space'=16] {'space'}, use_global_device_ids=true, to_apply=%region_2.3 | all-reduce | flops 4096 | bytes 32768 | tf_op jit(solution)/shard_map/psum | solution.py:59
  161.0 5.8 %cholesky.16 = f32[64,64]{1,0:T(8,128)S(1)} custom-call(f32[64,64]{1,0:T(8,128)S(1)} %fusion.84), custom_call_target="Cholesky" | custom-call | tf_op jit(solution)/shard_map/jit(cholesky)/cholesky | solution.py:60
  168.2 4.9 %custom-call.7 = f32[1,64,64]{1,2,0:T(8,128)S(1)} custom-call(f32[1,64,64]{2,1,0:T(8,128)S(1)} %fusion.82), custom_call_target="InvertDiagBlocksLowerTriangular" | custom-call | tf_op jit(solution)/shard_map/jit(_solve_triangular)/triangular_solve | solution.py:61
  173.1 1.5 convolution_convert_fusion
  174.6 1.0 copy.53
  (50 shorter events, 7.2 us)
Async XLA Ops:
  1.3 7.2 %collective-permute-start = (s32[1,128]{1,0:T(1,128)S(1)}, s32[1,128]{1,0:T(1,128)S(1)}, u32[]{:S(2)}, u32[]{:S(2)}) collective-permute-start(s32[1,128]{1,0:T(1,128)S(1)} %get-tuple-element.19), channel_id=1, source_target_pairs={{0,1},{1,2},{2,3},{3,4},{4,5},{5,6},{6,7},{7,8},{8,9},{9,10},{10,1... | collective-permute-start | bytes 1544 | tf_op jit(solution)/shard_map/ppermute | solution.py:17
  1.8 6.7 %collective-permute-start.1 = (s32[1,128]{1,0:T(1,128)S(1)}, s32[1,128]{1,0:T(1,128)S(1)}, u32[]{:S(2)}, u32[]{:S(2)}) collective-permute-start(s32[1,128]{1,0:T(1,128)S(1)} %get-tuple-element.20), channel_id=1, source_target_pairs={{1,0},{2,1},{3,2},{4,3},{5,4},{6,5},{7,6},{8,7},{9,8},{10,9},{11,1... | collective-permute-start | bytes 1544 | tf_op jit(solution)/shard_map/ppermute | solution.py:19
  7.8 2.2 %collective-permute-start.2 = (f32[16,3,1,128]{3,0,2,1:T(8,128)S(1)}, f32[16,3,1,128]{3,0,2,1:T(8,128)S(1)}, u32[]{:S(2)}, u32[]{:S(2)}) collective-permute-start(f32[16,3,1,128]{3,0,2,1:T(8,128)S(1)} %get-tuple-element.12), channel_id=1, source_target_pairs={{1,0},{2,1},{3,2},{4,3},{5,4},{6,5},{7,6},{8,7},{9,8},{10,9},{11,1... | collective-permute-start | bytes 73736 | tf_op jit(solution)/shard_map/ppermute | solution.py:19
  8.5 5.9 %collective-permute-start.3 = (f32[16,3,1,128]{3,0,2,1:T(8,128)S(1)}, f32[16,3,1,128]{3,0,2,1:T(8,128)S(1)}, u32[]{:S(2)}, u32[]{:S(2)}) collective-permute-start(f32[16,3,1,128]{3,0,2,1:T(8,128)S(1)} %get-tuple-element.13), channel_id=1, source_target_pairs={{0,1},{1,2},{2,3},{3,4},{4,5},{5,6},{6,7},{7,8},{8,9},{9,10},{10,1... | collective-permute-start | bytes 73736 | tf_op jit(solution)/shard_map/ppermute | solution.py:17
  15.7 1.6 collective-permute-start.4
  15.8 6.1 %collective-permute-start.5 = (f32[16,3,1,128]{3,0,2,1:T(8,128)S(1)}, f32[16,3,1,128]{3,0,2,1:T(8,128)S(1)}, u32[]{:S(2)}, u32[]{:S(2)}) collective-permute-start(f32[16,3,1,128]{3,0,2,1:T(8,128)S(1)} %get-tuple-element.11), channel_id=1, source_target_pairs={{0,1},{1,2},{2,3},{3,4},{4,5},{5,6},{6,7},{7,8},{8,9},{9,10},{10,1... | collective-permute-start | bytes 73736 | tf_op jit(solution)/shard_map/ppermute | solution.py:17
  22.1 19.9 %copy-start.2 = (s32[16,128]{1,0:T(8,128)S(1)}, s32[16,128]{1,0:T(8,128)}, u32[]{:S(2)}) copy-start(s32[16,128]{1,0:T(8,128)} %param.9) | copy-start | bytes 24580
  22.1 1.6 collective-permute-start.6
  22.2 6.1 %collective-permute-start.7 = (f32[16,3,1,128]{3,0,2,1:T(8,128)S(1)}, f32[16,3,1,128]{3,0,2,1:T(8,128)S(1)}, u32[]{:S(2)}, u32[]{:S(2)}) collective-permute-start(f32[16,3,1,128]{3,0,2,1:T(8,128)S(1)} %get-tuple-element.9), channel_id=1, source_target_pairs={{0,1},{1,2},{2,3},{3,4},{4,5},{5,6},{6,7},{7,8},{8,9},{9,10},{10,1... | collective-permute-start | bytes 73736 | tf_op jit(solution)/shard_map/ppermute | solution.py:17
  28.6 1.6 collective-permute-start.8
  28.6 6.1 %collective-permute-start.9 = (f32[16,3,1,128]{3,0,2,1:T(8,128)S(1)}, f32[16,3,1,128]{3,0,2,1:T(8,128)S(1)}, u32[]{:S(2)}, u32[]{:S(2)}) collective-permute-start(f32[16,3,1,128]{3,0,2,1:T(8,128)S(1)} %get-tuple-element.7), channel_id=1, source_target_pairs={{0,1},{1,2},{2,3},{3,4},{4,5},{5,6},{6,7},{7,8},{8,9},{9,10},{10,1... | collective-permute-start | bytes 73736 | tf_op jit(solution)/shard_map/ppermute | solution.py:17
  35.0 1.6 collective-permute-start.10
  35.1 6.1 %collective-permute-start.11 = (f32[16,3,1,128]{3,0,2,1:T(8,128)S(1)}, f32[16,3,1,128]{3,0,2,1:T(8,128)S(1)}, u32[]{:S(2)}, u32[]{:S(2)}) collective-permute-start(f32[16,3,1,128]{3,0,2,1:T(8,128)S(1)} %get-tuple-element.5), channel_id=1, source_target_pairs={{0,1},{1,2},{2,3},{3,4},{4,5},{5,6},{6,7},{7,8},{8,9},{9,10},{10,1... | collective-permute-start | bytes 73736 | tf_op jit(solution)/shard_map/ppermute | solution.py:17
  41.4 1.6 collective-permute-start.12
  41.5 6.0 %collective-permute-start.13 = (f32[16,3,1,128]{3,0,2,1:T(8,128)S(1)}, f32[16,3,1,128]{3,0,2,1:T(8,128)S(1)}, u32[]{:S(2)}, u32[]{:S(2)}) collective-permute-start(f32[16,3,1,128]{3,0,2,1:T(8,128)S(1)} %get-tuple-element.3), channel_id=1, source_target_pairs={{0,1},{1,2},{2,3},{3,4},{4,5},{5,6},{6,7},{7,8},{8,9},{9,10},{10,1... | collective-permute-start | bytes 73736 | tf_op jit(solution)/shard_map/ppermute | solution.py:17
  47.8 7.0 %copy-start = (bf16[64,3,8,256]{3,2,1,0:T(8,128)(2,1)S(1)}, bf16[64,3,8,256]{3,2,1,0:T(8,128)(2,1)}, u32[]{:S(2)}) copy-start(bf16[64,3,8,256]{3,2,1,0:T(8,128)(2,1)} %param.7) | copy-start | bytes 2359300
  51.2 12.5 %all-to-all-start = ((bf16[16,2,3072]{2,1,0:T(2,128)(2,1)}), bf16[16,2,3072]{2,1,0:T(2,128)(2,1)S(1)}, u32[]{:S(2)}, u32[]{:S(2)}) async-start(bf16[16,2,3072]{2,1,0:T(2,128)(2,1)} %reshape.52), calls=%async_computation | async-start | bytes 393216 | tf_op jit(solution)/shard_map/all_to_all | solution.py:79
  67.1 2.7 %copy-start.1 = (bf16[64,3,8,256]{3,2,1,0:T(8,128)(2,1)S(1)}, bf16[64,3,8,256]{3,2,1,0:T(8,128)(2,1)}, u32[]{:S(2)}) copy-start(bf16[64,3,8,256]{3,2,1,0:T(8,128)(2,1)} %param.7) | copy-start | bytes 2359300
  67.1 34.0 %copy-start.4 = (f32[64]{0:T(128)S(1)}, f32[64]{0:T(128)}, u32[]{:S(2)}) copy-start(f32[64]{0:T(128)} %param.8) | copy-start | bytes 772
  101.1 0.6 copy-start.3
where the time goes:
time: 176 us
  blocking collectives  88.8 us (50%)
  waiting for transfers between devices  41 us (23%)
  other arithmetic  17.2 us (10%)
  starting transfers between devices  12.5 us (7%)
  local copies, waits for them, and re-layouts  11.7 us (7%)
  matrix products  3.56 us (2%)
    psum x1, blocking collectives, eof_update(): lax.psum(jnp.dot(update, update.T, precision=high), 'space') / total_cells  57.8 us
    psum x1, blocking collectives, eof_update(): cross_sum = lax.psum(dot_rows(data_rows, basis_rows), 'space')  31 us
    ppermute x7, waiting for transfers between devices, with_halo(): lax.ppermute(tail, axis, [(i, (i + 1) % count) for i in range(count)])  27.1 us
    all_to_all x1, waiting for transfers between devices, local(): lax.all_to_all(filtered, 'space', split_axis=3, concat_axis=2, tiled=True)  8.79 us
    another operation x3, other arithmetic, eof_update(): chol_factor = jnp.linalg.cholesky(gram_matrix)  6.52 us
    ppermute x7, starting transfers between devices, with_halo(): lax.ppermute(head, axis, [((i + 1) % count, i) for i in range(count)])  6.01 us
    another operation x2, other arithmetic, eof_update(): solved = jax.scipy.linalg.solve_triangular(chol_factor, update, lower=True)  5.55 us
    ppermute x7, waiting for transfers between devices, with_halo(): lax.ppermute(head, axis, [((i + 1) % count, i) for i in range(count)])  5.11 us
  transfers between devices with their start and end apart: 15, of which 12 were waited for; matrix products, arithmetic and copies ran while one was open for 1% of the time, Pallas kernels for 0%

commit v1 on v0

--- a/solution.py
+++ b/solution.py
@@ -76,7 +76,12 @@
     filtered = (ocean * fields_now).astype(jnp.bfloat16)
     modes = basis.shape[0]
     snaps = filtered.shape[0]
-    slab_data = lax.all_to_all(filtered, "space", split_axis=3, concat_axis=2, tiled=True)
+    slab_data = jnp.concatenate(
+        lax.all_to_all(
+            jnp.stack(jnp.split(filtered, lax.axis_size("space"), axis=3)), "space", 0, 0
+        ),
+        axis=2,
+    )
     data_rows = jnp.swapaxes(slab_data, 2, 3).reshape(snaps, -1)
     basis_rows = basis.reshape(modes, -1)
     total_cells = float(data_rows.shape[1] * lax.axis_size("space"))

time: 176 us -> 191 us (1.085)
  local copies, waits for them, and re-layouts: 11.7 us -> 25.2 us
    unnamed x15 -> x28, local copies, waits for them, and re-layouts: 4.89 us -> 16.6 us
    another operation x0 -> x2, local copies, waits for them, and re-layouts: none -> 4.91 us  [local(): jnp.stack(jnp.split(filtered, lax.axis_size('space'), axis=3))]
    all_to_all x2 -> x0, local copies, waits for them, and re-layouts: 4.88 us -> none  [local(): lax.all_to_all(filtered, 'space', split_axis=3, concat_axis=2, tiled=True)]
    reshape x0 -> x3, local copies, waits for them, and re-layouts: none -> 2.78 us  [local(): jnp.concatenate(lax.all_to_all(jnp.stack(jnp.split(filtered, lax.axis_siz...]
where the time goes in v1:
time: 191 us; the launch traced here: 190 us
  blocking collectives  88.6 us (46%)
  waiting for transfers between devices  40.8 us (21%)
  local copies, waits for them, and re-layouts  25.2 us (13%)
  other arithmetic  17.2 us (9%)
  starting transfers between devices  12.7 us (7%)
  matrix products  4.7 us (2%)
    psum x1, blocking collectives, eof_update(): lax.psum(jnp.dot(update, update.T, precision=high), 'space') / total_cells  57.6 us
    psum x1, blocking collectives, eof_update(): cross_sum = lax.psum(dot_rows(data_rows, basis_rows), 'space')  31 us
    ppermute x7, waiting for transfers between devices, with_halo(): lax.ppermute(tail, axis, [(i, (i + 1) % count) for i in range(count)])  27.1 us
    unnamed x28, local copies, waits for them, and re-layouts  16.6 us
    all_to_all x1, waiting for transfers between devices, local(): lax.all_to_all(jnp.stack(jnp.split(filtered, lax.axis_size('space'), axis...  8.61 us
    another operation x3, other arithmetic, eof_update(): chol_factor = jnp.linalg.cholesky(gram_matrix)  6.52 us
    ppermute x7, starting transfers between devices, with_halo(): lax.ppermute(head, axis, [((i + 1) % count, i) for i in range(count)])  6.01 us
    another operation x2, other arithmetic, eof_update(): solved = jax.scipy.linalg.solve_triangular(chol_factor, update, lower=True)  5.55 us
  transfers between devices with their start and end apart: 15, of which 12 were waited for; matrix products, arithmetic and copies ran while one was open for 1% of the time, Pallas kernels for 0%

profile of v1, /device:TPU:0, one launch (start us, length us, event | category | flops | bytes accessed | tf_op | source)
XLA Modules:
  0.0 190.1 jit_solution(1905773476670101564)
XLA Ops:
  1.9 5.0 %collective-permute-start.1 = (s32[1,128]{1,0:T(1,128)S(1)}, s32[1,128]{1,0:T(1,128)S(1)}, u32[]{:S(2)}, u32[]{:S(2)}) collective-permute-start(s32[1,128]{1,0:T(1,128)S(1)} %get-tuple-element.20), channel_id=1, source_target_pairs={{1,0},{2,1},{3,2},{4,3},{5,4},{6,5},{7,6},{8,7},{9,8},{10,9},{11,1... | collective-permute-start | bytes 1544 | tf_op jit(solution)/shard_map/ppermute | solution.py:19
  6.8 1.0 copy_convert_fusion
  10.1 4.4 %collective-permute-done.3 = f32[16,3,1,128]{3,0,2,1:T(8,128)S(1)} collective-permute-done((f32[16,3,1,128]{3,0,2,1:T(8,128)S(1)}, f32[16,3,1,128]{3,0,2,1:T(8,128)S(1)}, u32[]{:S(2)}, u32[]{:S(2)}) %collective-permute-start.3) | collective-permute-done | bytes 24608 | tf_op jit(solution)/shard_map/ppermute | solution.py:17
  14.5 1.2 convert_add_fusion
  16.3 1.0 collective-permute-done.4
  17.3 4.5 %collective-permute-done.5 = f32[16,3,1,128]{3,0,2,1:T(8,128)S(1)} collective-permute-done((f32[16,3,1,128]{3,0,2,1:T(8,128)S(1)}, f32[16,3,1,128]{3,0,2,1:T(8,128)S(1)}, u32[]{:S(2)}, u32[]{:S(2)}) %collective-permute-start.5) | collective-permute-done | bytes 24608 | tf_op jit(solution)/shard_map/ppermute | solution.py:17
  22.7 1.0 collective-permute-done.6
  23.7 4.5 %collective-permute-done.7 = f32[16,3,1,128]{3,0,2,1:T(8,128)S(1)} collective-permute-done((f32[16,3,1,128]{3,0,2,1:T(8,128)S(1)}, f32[16,3,1,128]{3,0,2,1:T(8,128)S(1)}, u32[]{:S(2)}, u32[]{:S(2)}) %collective-permute-start.7) | collective-permute-done | bytes 24608 | tf_op jit(solution)/shard_map/ppermute | solution.py:17
  29.2 1.0 collective-permute-done.8
  30.2 4.5 %collective-permute-done.9 = f32[16,3,1,128]{3,0,2,1:T(8,128)S(1)} collective-permute-done((f32[16,3,1,128]{3,0,2,1:T(8,128)S(1)}, f32[16,3,1,128]{3,0,2,1:T(8,128)S(1)}, u32[]{:S(2)}, u32[]{:S(2)}) %collective-permute-start.9) | collective-permute-done | bytes 24608 | tf_op jit(solution)/shard_map/ppermute | solution.py:17
  35.6 1.0 collective-permute-done.10
  36.6 4.5 %collective-permute-done.11 = f32[16,3,1,128]{3,0,2,1:T(8,128)S(1)} collective-permute-done((f32[16,3,1,128]{3,0,2,1:T(8,128)S(1)}, f32[16,3,1,128]{3,0,2,1:T(8,128)S(1)}, u32[]{:S(2)}, u32[]{:S(2)}) %collective-permute-start.11) | collective-permute-done | bytes 24608 | tf_op jit(solution)/shard_map/ppermute | solution.py:17
  42.0 1.0 collective-permute-done.12
  43.0 4.5 %collective-permute-done.13 = f32[16,3,1,128]{3,0,2,1:T(8,128)S(1)} collective-permute-done((f32[16,3,1,128]{3,0,2,1:T(8,128)S(1)}, f32[16,3,1,128]{3,0,2,1:T(8,128)S(1)}, u32[]{:S(2)}, u32[]{:S(2)}) %collective-permute-start.13) | collective-permute-done | bytes 24608 | tf_op jit(solution)/shard_map/ppermute | solution.py:17
  50.9 0.8 fusion.93
  52.5 0.8 fusion.91
  58.9 0.8 fusion.83
  60.5 4.1 %copy.37 = bf16[16,16,3,16,8]{3,4,2,1,0:T(8,128)(2,1)S(1)} copy(bf16[16,16,3,16,8]{4,1,3,2,0:T(8,128)(2,1)} %fusion.82) | data formatting | bytes 393216 | tf_op jit(solution)/shard_map/stack | solution.py:81
  64.6 2.3 %reshape.60 = bf16[16,2,3072]{2,1,0:T(2,128)(2,1)} reshape(bf16[16,16,3,8,16]{4,3,2,1,0:T(8,128)(2,1)S(1)} %bitcast.106) | data formatting | bytes 393216
  67.0 3.7 %all-to-all-start = ((bf16[16,2,3072]{2,1,0:T(2,128)(2,1)}), bf16[16,2,3072]{2,1,0:T(2,128)(2,1)S(1)}, u32[]{:S(2)}, u32[]{:S(2)}) async-start(bf16[16,2,3072]{2,1,0:T(2,128)(2,1)} %reshape.60), calls=%async_computation | async-start | bytes 393216 | tf_op jit(solution)/shard_map/all_to_all | solution.py:80
  70.9 8.6 %all-to-all-done = bf16[16,2,3072]{2,1,0:T(2,128)(2,1)S(1)} async-done(((bf16[16,2,3072]{2,1,0:T(2,128)(2,1)}), bf16[16,2,3072]{2,1,0:T(2,128)(2,1)S(1)}, u32[]{:S(2)}, u32[]{:S(2)}) %all-to-all-start) | async-done | bytes 196640 | tf_op jit(solution)/shard_map/all_to_all | solution.py:80
  79.5 1.2 reshape.61
  80.9 1.0 copy.38
  82.0 1.5 reshape.55
  83.5 1.4 convolution_bitcast_fusion
  84.9 31.0 %psum.14 = f32[16,64]{1,0:T(8,128)S(1)} all-reduce(f32[16,64]{1,0:T(8,128)S(1)} %convolution_bitcast_fusion), channel_id=1, replica_groups=mesh['group'=2,'space'=16] {'space'}, use_global_device_ids=true, to_apply=%region_1.2 | all-reduce | flops 1024 | bytes 8192 | tf_op jit(solution)/shard_map/psum | solution.py:53
  116.4 1.4 fusion.111
  117.8 57.6 %psum.15 = f32[64,64]{0,1:T(8,128)S(1)} all-reduce(f32[64,64]{0,1:T(8,128)S(1)} %fusion.111), channel_id=1, replica_groups=mesh['group'=2,'space'=16] {'space'}, use_global_device_ids=true, to_apply=%region_2.3 | all-reduce | flops 4096 | bytes 32768 | tf_op jit(solution)/shard_map/psum | solution.py:59
  175.5 5.8 %cholesky.16 = f32[64,64]{1,0:T(8,128)S(1)} custom-call(f32[64,64]{1,0:T(8,128)S(1)} %fusion.100), custom_call_target="Cholesky" | custom-call | tf_op jit(solution)/shard_map/jit(cholesky)/cholesky | solution.py:60
  182.7 4.9 %custom-call.7 = f32[1,64,64]{1,2,0:T(8,128)S(1)} custom-call(f32[1,64,64]{2,1,0:T(8,128)S(1)} %fusion.98), custom_call_target="InvertDiagBlocksLowerTriangular" | custom-call | tf_op jit(solution)/shard_map/jit(_solve_triangular)/triangular_solve | solution.py:61
  187.6 1.5 convolution_convert_fusion
  189.1 1.0 copy.47
  (65 shorter events, 20.2 us)
Async XLA Ops:
  0.6 41.4 %copy-start.1 = (s32[16,128]{1,0:T(8,128)S(1)}, s32[16,128]{1,0:T(8,128)}, u32[]{:S(2)}) copy-start(s32[16,128]{1,0:T(8,128)} %param.9) | copy-start | bytes 24580
  1.4 7.2 %collective-permute-start = (s32[1,128]{1,0:T(1,128)S(1)}, s32[1,128]{1,0:T(1,128)S(1)}, u32[]{:S(2)}, u32[]{:S(2)}) collective-permute-start(s32[1,128]{1,0:T(1,128)S(1)} %get-tuple-element.19), channel_id=1, source_target_pairs={{0,1},{1,2},{2,3},{3,4},{4,5},{5,6},{6,7},{7,8},{8,9},{9,10},{10,1... | collective-permute-start | bytes 1544 | tf_op jit(solution)/shard_map/ppermute | solution.py:17
  1.9 6.7 %collective-permute-start.1 = (s32[1,128]{1,0:T(1,128)S(1)}, s32[1,128]{1,0:T(1,128)S(1)}, u32[]{:S(2)}, u32[]{:S(2)}) collective-permute-start(s32[1,128]{1,0:T(1,128)S(1)} %get-tuple-element.20), channel_id=1, source_target_pairs={{1,0},{2,1},{3,2},{4,3},{5,4},{6,5},{7,6},{8,7},{9,8},{10,9},{11,1... | collective-permute-start | bytes 1544 | tf_op jit(solution)/shard_map/ppermute | solution.py:19
  7.8 2.2 %collective-permute-start.2 = (f32[16,3,1,128]{3,0,2,1:T(8,128)S(1)}, f32[16,3,1,128]{3,0,2,1:T(8,128)S(1)}, u32[]{:S(2)}, u32[]{:S(2)}) collective-permute-start(f32[16,3,1,128]{3,0,2,1:T(8,128)S(1)} %get-tuple-element.12), channel_id=1, source_target_pairs={{1,0},{2,1},{3,2},{4,3},{5,4},{6,5},{7,6},{8,7},{9,8},{10,9},{11,1... | collective-permute-start | bytes 73736 | tf_op jit(solution)/shard_map/ppermute | solution.py:19
  8.6 5.9 %collective-permute-start.3 = (f32[16,3,1,128]{3,0,2,1:T(8,128)S(1)}, f32[16,3,1,128]{3,0,2,1:T(8,128)S(1)}, u32[]{:S(2)}, u32[]{:S(2)}) collective-permute-start(f32[16,3,1,128]{3,0,2,1:T(8,128)S(1)} %get-tuple-element.13), channel_id=1, source_target_pairs={{0,1},{1,2},{2,3},{3,4},{4,5},{5,6},{6,7},{7,8},{8,9},{9,10},{10,1... | collective-permute-start | bytes 73736 | tf_op jit(solution)/shard_map/ppermute | solution.py:17
  15.7 1.6 collective-permute-start.4
  15.8 6.1 %collective-permute-start.5 = (f32[16,3,1,128]{3,0,2,1:T(8,128)S(1)}, f32[16,3,1,128]{3,0,2,1:T(8,128)S(1)}, u32[]{:S(2)}, u32[]{:S(2)}) collective-permute-start(f32[16,3,1,128]{3,0,2,1:T(8,128)S(1)} %get-tuple-element.11), channel_id=1, source_target_pairs={{0,1},{1,2},{2,3},{3,4},{4,5},{5,6},{6,7},{7,8},{8,9},{9,10},{10,1... | collective-permute-start | bytes 73736 | tf_op jit(solution)/shard_map/ppermute | solution.py:17
  22.2 1.6 collective-permute-start.6
  22.2 6.1 %collective-permute-start.7 = (f32[16,3,1,128]{3,0,2,1:T(8,128)S(1)}, f32[16,3,1,128]{3,0,2,1:T(8,128)S(1)}, u32[]{:S(2)}, u32[]{:S(2)}) collective-permute-start(f32[16,3,1,128]{3,0,2,1:T(8,128)S(1)} %get-tuple-element.9), channel_id=1, source_target_pairs={{0,1},{1,2},{2,3},{3,4},{4,5},{5,6},{6,7},{7,8},{8,9},{9,10},{10,1... | collective-permute-start | bytes 73736 | tf_op jit(solution)/shard_map/ppermute | solution.py:17
  28.6 1.6 collective-permute-start.8
  28.7 6.1 %collective-permute-start.9 = (f32[16,3,1,128]{3,0,2,1:T(8,128)S(1)}, f32[16,3,1,128]{3,0,2,1:T(8,128)S(1)}, u32[]{:S(2)}, u32[]{:S(2)}) collective-permute-start(f32[16,3,1,128]{3,0,2,1:T(8,128)S(1)} %get-tuple-element.7), channel_id=1, source_target_pairs={{0,1},{1,2},{2,3},{3,4},{4,5},{5,6},{6,7},{7,8},{8,9},{9,10},{10,1... | collective-permute-start | bytes 73736 | tf_op jit(solution)/shard_map/ppermute | solution.py:17
  35.0 1.6 collective-permute-start.10
  35.1 6.1 %collective-permute-start.11 = (f32[16,3,1,128]{3,0,2,1:T(8,128)S(1)}, f32[16,3,1,128]{3,0,2,1:T(8,128)S(1)}, u32[]{:S(2)}, u32[]{:S(2)}) collective-permute-start(f32[16,3,1,128]{3,0,2,1:T(8,128)S(1)} %get-tuple-element.5), channel_id=1, source_target_pairs={{0,1},{1,2},{2,3},{3,4},{4,5},{5,6},{6,7},{7,8},{8,9},{9,10},{10,1... | collective-permute-start | bytes 73736 | tf_op jit(solution)/shard_map/ppermute | solution.py:17
  41.4 1.6 collective-permute-start.12
  41.5 6.0 %collective-permute-start.13 = (f32[16,3,1,128]{3,0,2,1:T(8,128)S(1)}, f32[16,3,1,128]{3,0,2,1:T(8,128)S(1)}, u32[]{:S(2)}, u32[]{:S(2)}) collective-permute-start(f32[16,3,1,128]{3,0,2,1:T(8,128)S(1)} %get-tuple-element.3), channel_id=1, source_target_pairs={{0,1},{1,2},{2,3},{3,4},{4,5},{5,6},{6,7},{7,8},{8,9},{9,10},{10,1... | collective-permute-start | bytes 73736 | tf_op jit(solution)/shard_map/ppermute | solution.py:17
  60.5 10.2 %copy-start = (bf16[64,3,8,256]{3,2,1,0:T(8,128)(2,1)S(1)}, bf16[64,3,8,256]{3,2,1,0:T(8,128)(2,1)}, u32[]{:S(2)}) copy-start(bf16[64,3,8,256]{3,2,1,0:T(8,128)(2,1)} %param.7) | copy-start | bytes 2359300
  67.0 12.5 %all-to-all-start = ((bf16[16,2,3072]{2,1,0:T(2,128)(2,1)}), bf16[16,2,3072]{2,1,0:T(2,128)(2,1)S(1)}, u32[]{:S(2)}, u32[]{:S(2)}) async-start(bf16[16,2,3072]{2,1,0:T(2,128)(2,1)} %reshape.60), calls=%async_computation | async-start | bytes 393216 | tf_op jit(solution)/shard_map/all_to_all | solution.py:80
  80.9 35.1 %copy-start.3 = (f32[64]{0:T(128)S(1)}, f32[64]{0:T(128)}, u32[]{:S(2)}) copy-start(f32[64]{0:T(128)} %param.8) | copy-start | bytes 772
  116.0 1.8 copy-start.2
